TPU v7x, 32 devices: a whole 2x2x4 slice. The times are simulated.
32 devices in a mesh: row: 4 (over x, core), col: 8 (over z, y).
Axes of the slice: x: 2, y: 2, z: 4, core: 2. Of those that a mesh axis runs over, the one named last changes fastest.
Arguments:
- rhs: float32 [24, 32768], P(None, 'col'), may hold values from -6 to 6
- noise_var: float32 [32768], P('col'), may hold values from 0.9 to 3.6
- block_rows: int32 [4, 4], P('row'), may hold values from 0 to 15, as said below
- kernel_blocks: bfloat16 [4, 8, 4, 2, 2048, 2048], P('row', 'col'), may hold values from -0.0078125 to 0.0078125
Outputs:
- solution_field: float32 [24, 32768], P(None, 'col')
- residual: float32 [24, 32768], P(None, 'col')
Inputs may be any that keep to these rules, and one draw needn't show every extreme that they name: Each of the 16 block rows appears exactly once in block_rows.
All inputs are finite; a program needn't handle non-finite values.
Results may differ from a plain program's by a relative error of at most 0.024.
Values may be sent and summed in bfloat16 or wider, within the bound.
A program may use at most 192 MiB of HBM per device.

v0:
```python
import jax
import jax.numpy as jnp
from jax import lax
from jax.sharding import PartitionSpec as P

ITERS = 8


def fetch_rows(slab_bf, row_blocks, width):
    pieces = []
    gathered = lax.all_gather(slab_bf, "col", axis=1, tiled=True)
    for k in range(row_blocks.shape[0]):
        pieces.append(lax.dynamic_slice_in_dim(gathered, row_blocks[k] * width, width, 1))
    return pieces


def kernel_terms(slab_bf, row_blocks, blocks):
    col_blocks = blocks.shape[1]
    width = blocks.shape[2]
    vectors = slab_bf.shape[0]
    col_ids = lax.axis_index("col") * col_blocks + jnp.arange(col_blocks, dtype=jnp.int32)
    fetched = fetch_rows(slab_bf, row_blocks, width)
    forward_list = []
    mirrored = [jnp.zeros((vectors, width), jnp.float32) for m in range(col_blocks)]
    for k in range(row_blocks.shape[0]):
        forward_sum = jnp.zeros((vectors, width), jnp.float32)
        for m in range(col_blocks):
            used = col_ids[m] >= row_blocks[k]
            col_piece = slab_bf[:, m * width : (m + 1) * width]
            forward = lax.dot_general(
                col_piece,
                blocks[k, m],
                (((1,), (1,)), ((), ())),
                preferred_element_type=jnp.float32,
            )
            forward_sum = forward_sum + jnp.where(used, forward, 0.0)
            product = jnp.dot(fetched[k], blocks[k, m], preferred_element_type=jnp.float32)
            mirrored[m] = mirrored[m] + jnp.where(used, product, 0.0)
        forward_list.append(forward_sum)
    row_sums = lax.psum(jnp.stack(forward_list).astype(jnp.bfloat16), "col").astype(jnp.float32)
    terms = jnp.stack(mirrored, axis=1)
    for k in range(row_blocks.shape[0]):
        select = (col_ids == row_blocks[k]).astype(jnp.float32)
        terms = terms + select[None, :, None] * row_sums[k][:, None, :]
    return terms.reshape(vectors, col_blocks * width)


def slab_total(value):
    return lax.psum(value, "col")


def on_device(rhs, noise_var, block_rows, kernel_blocks):
    blocks = kernel_blocks[0, 0]
    row_blocks = block_rows[0]
    solution = jnp.zeros_like(rhs)
    residual = rhs
    direction = rhs
    norm_now = slab_total(jnp.sum(residual * residual, axis=1))
    for step in range(ITERS):
        terms = kernel_terms(direction.astype(jnp.bfloat16), row_blocks, blocks)
        image = noise_var[None, :] * direction + lax.psum(terms, "row")
        curvature = slab_total(jnp.sum(direction * image, axis=1))
        alpha = norm_now / curvature
        solution = solution + alpha[:, None] * direction
        residual = residual - alpha[:, None] * image
        norm_next = slab_total(jnp.sum(residual * residual, axis=1))
        direction = residual + (norm_next / norm_now)[:, None] * direction
        norm_now = norm_next
    return (solution, residual)


def solution(mesh):
    return jax.shard_map(
        on_device,
        mesh=mesh,
        in_specs=(
            P(None, "col"),
            P("col"),
            P("row", None),
            P("row", "col", None, None, None, None),
        ),
        out_specs=(P(None, "col"), P(None, "col")),
        check_vma=False,
    )
```

profile of v0, /device:TPU:0, one launch (start us, length us, event | category | flops | bytes accessed | tf_op | source)
XLA Modules:
  0.0 2201.9 jit_solution(17760173338143763754)
XLA Ops:
  73.3 68.1 %all-reduce.18.cloned.1.call-done = bf16[4,24,2048]{2,1,0:T(8,128)(2,1)} async-done(((bf16[4,24,2048]{2,1,0:T(8,128)(2,1)}), bf16[4,24,2048]{2,1,0:T(8,128)(2,1)}) %all-reduce.18.cloned.1.call-update) | async-done | bytes 393232 | tf_op jit(solution)/shard_map/psum | solution.py:40
  144.3 43.4 %all-gather.9.cloned.1.call-done = bf16[24,32768]{1,0:T(8,128)(2,1)} async-done(((bf16[24,4096]{1,0:T(8,128)(2,1)}), bf16[24,32768]{1,0:T(8,128)(2,1)}) %all-gather.9.cloned.1.call-update) | async-done | bytes 1572880 | tf_op jit(solution)/shard_map/all_gather | solution.py:11
  225.9 31.5 %all-reduce.20.cloned.1.call-done = f32[24,4096]{1,0:T(8,128)} async-done(((f32[24,4096]{1,0:T(8,128)}), f32[24,4096]{1,0:T(8,128)}) %all-reduce.20.cloned.1.call-update) | async-done | bytes 393232 | tf_op jit(solution)/shard_map/psum | solution.py:61
  258.6 21.4 all-reduce
  347.0 68.6 %all-reduce.22.cloned.1.call-done = bf16[4,24,2048]{2,1,0:T(8,128)(2,1)} async-done(((bf16[4,24,2048]{2,1,0:T(8,128)(2,1)}), bf16[4,24,2048]{2,1,0:T(8,128)(2,1)}) %all-reduce.22.cloned.1.call-update) | async-done | bytes 393232 | tf_op jit(solution)/shard_map/psum | solution.py:40
  418.5 43.2 %all-gather.11.cloned.1.call-done = bf16[24,32768]{1,0:T(8,128)(2,1)} async-done(((bf16[24,4096]{1,0:T(8,128)(2,1)}), bf16[24,32768]{1,0:T(8,128)(2,1)}) %all-gather.11.cloned.1.call-update) | async-done | bytes 1572880 | tf_op jit(solution)/shard_map/all_gather | solution.py:11
  500.0 31.5 %all-reduce.24.cloned.1.call-done = f32[24,4096]{1,0:T(8,128)} async-done(((f32[24,4096]{1,0:T(8,128)}), f32[24,4096]{1,0:T(8,128)}) %all-reduce.24.cloned.1.call-update) | async-done | bytes 393232 | tf_op jit(solution)/shard_map/psum | solution.py:61
  532.8 21.4 psum.231
  620.6 68.4 %all-reduce.26.cloned.1.call-done = bf16[4,24,2048]{2,1,0:T(8,128)(2,1)} async-done(((bf16[4,24,2048]{2,1,0:T(8,128)(2,1)}), bf16[4,24,2048]{2,1,0:T(8,128)(2,1)}) %all-reduce.26.cloned.1.call-update) | async-done | bytes 393232 | tf_op jit(solution)/shard_map/psum | solution.py:40
  692.0 43.4 %all-gather.13.cloned.1.call-done = bf16[24,32768]{1,0:T(8,128)(2,1)} async-done(((bf16[24,4096]{1,0:T(8,128)(2,1)}), bf16[24,32768]{1,0:T(8,128)(2,1)}) %all-gather.13.cloned.1.call-update) | async-done | bytes 1572880 | tf_op jit(solution)/shard_map/all_gather | solution.py:11
  773.6 31.5 %all-reduce.28.cloned.1.call-done = f32[24,4096]{1,0:T(8,128)} async-done(((f32[24,4096]{1,0:T(8,128)}), f32[24,4096]{1,0:T(8,128)}) %all-reduce.28.cloned.1.call-update) | async-done | bytes 393232 | tf_op jit(solution)/shard_map/psum | solution.py:61
  806.3 21.4 psum.235
  893.9 68.5 %all-reduce.30.cloned.1.call-done = bf16[4,24,2048]{2,1,0:T(8,128)(2,1)} async-done(((bf16[4,24,2048]{2,1,0:T(8,128)(2,1)}), bf16[4,24,2048]{2,1,0:T(8,128)(2,1)}) %all-reduce.30.cloned.1.call-update) | async-done | bytes 393232 | tf_op jit(solution)/shard_map/psum | solution.py:40
  965.3 42.8 %all-gather.15.cloned.1.call-done = bf16[24,32768]{1,0:T(8,128)(2,1)} async-done(((bf16[24,4096]{1,0:T(8,128)(2,1)}), bf16[24,32768]{1,0:T(8,128)(2,1)}) %all-gather.15.cloned.1.call-update) | async-done | bytes 1572880 | tf_op jit(solution)/shard_map/all_gather | solution.py:11
  1046.3 31.5 %all-reduce.32.cloned.1.call-done = f32[24,4096]{1,0:T(8,128)} async-done(((f32[24,4096]{1,0:T(8,128)}), f32[24,4096]{1,0:T(8,128)}) %all-reduce.32.cloned.1.call-update) | async-done | bytes 393232 | tf_op jit(solution)/shard_map/psum | solution.py:61
  1079.0 21.4 psum.239
  1166.4 68.6 %all-reduce.34.cloned.1.call-done = bf16[4,24,2048]{2,1,0:T(8,128)(2,1)} async-done(((bf16[4,24,2048]{2,1,0:T(8,128)(2,1)}), bf16[4,24,2048]{2,1,0:T(8,128)(2,1)}) %all-reduce.34.cloned.1.call-update) | async-done | bytes 393232 | tf_op jit(solution)/shard_map/psum | solution.py:40
  1237.9 42.6 %all-gather.17.cloned.1.call-done = bf16[24,32768]{1,0:T(8,128)(2,1)} async-done(((bf16[24,4096]{1,0:T(8,128)(2,1)}), bf16[24,32768]{1,0:T(8,128)(2,1)}) %all-gather.17.cloned.1.call-update) | async-done | bytes 1572880 | tf_op jit(solution)/shard_map/all_gather | solution.py:11
  1318.8 31.5 %all-reduce.36.cloned.1.call-done = f32[24,4096]{1,0:T(8,128)} async-done(((f32[24,4096]{1,0:T(8,128)}), f32[24,4096]{1,0:T(8,128)}) %all-reduce.36.cloned.1.call-update) | async-done | bytes 393232 | tf_op jit(solution)/shard_map/psum | solution.py:61
  1351.4 21.4 psum.243
  1438.8 68.6 %all-reduce.38.cloned.1.call-done = bf16[4,24,2048]{2,1,0:T(8,128)(2,1)} async-done(((bf16[4,24,2048]{2,1,0:T(8,128)(2,1)}), bf16[4,24,2048]{2,1,0:T(8,128)(2,1)}) %all-reduce.38.cloned.1.call-update) | async-done | bytes 393232 | tf_op jit(solution)/shard_map/psum | solution.py:40
  1510.3 42.6 %all-gather.19.cloned.1.call-done = bf16[24,32768]{1,0:T(8,128)(2,1)} async-done(((bf16[24,4096]{1,0:T(8,128)(2,1)}), bf16[24,32768]{1,0:T(8,128)(2,1)}) %all-gather.19.cloned.1.call-update) | async-done | bytes 1572880 | tf_op jit(solution)/shard_map/all_gather | solution.py:11
  1591.2 31.5 %all-reduce.40.cloned.1.call-done = f32[24,4096]{1,0:T(8,128)} async-done(((f32[24,4096]{1,0:T(8,128)}), f32[24,4096]{1,0:T(8,128)}) %all-reduce.40.cloned.1.call-update) | async-done | bytes 393232 | tf_op jit(solution)/shard_map/psum | solution.py:61
  1623.9 21.4 psum.247
  1711.2 68.6 %all-reduce.42.cloned.1.call-done = bf16[4,24,2048]{2,1,0:T(8,128)(2,1)} async-done(((bf16[4,24,2048]{2,1,0:T(8,128)(2,1)}), bf16[4,24,2048]{2,1,0:T(8,128)(2,1)}) %all-reduce.42.cloned.1.call-update) | async-done | bytes 393232 | tf_op jit(solution)/shard_map/psum | solution.py:40
  1782.8 42.6 %all-gather.21.cloned.1.call-done = bf16[24,32768]{1,0:T(8,128)(2,1)} async-done(((bf16[24,4096]{1,0:T(8,128)(2,1)}), bf16[24,32768]{1,0:T(8,128)(2,1)}) %all-gather.21.cloned.1.call-update) | async-done | bytes 1572880 | tf_op jit(solution)/shard_map/all_gather | solution.py:11
  1863.6 31.5 %all-reduce.44.cloned.1.call-done = f32[24,4096]{1,0:T(8,128)} async-done(((f32[24,4096]{1,0:T(8,128)}), f32[24,4096]{1,0:T(8,128)}) %all-reduce.44.cloned.1.call-update) | async-done | bytes 393232 | tf_op jit(solution)/shard_map/psum | solution.py:61
  1896.3 21.4 psum.251
  1983.7 68.2 %all-reduce.46.cloned.1.call-done = bf16[4,24,2048]{2,1,0:T(8,128)(2,1)} async-done(((bf16[4,24,2048]{2,1,0:T(8,128)(2,1)}), bf16[4,24,2048]{2,1,0:T(8,128)(2,1)}) %all-reduce.46.cloned.1.call-update) | async-done | bytes 393232 | tf_op jit(solution)/shard_map/psum | solution.py:40
  2057.1 40.6 %all-gather.23.cloned.1.call-done = bf16[24,32768]{1,0:T(8,128)(2,1)} async-done(((bf16[24,4096]{1,0:T(8,128)(2,1)}), bf16[24,32768]{1,0:T(8,128)(2,1)}) %all-gather.23.cloned.1.call-update) | async-done | bytes 1572880 | tf_op jit(solution)/shard_map/all_gather | solution.py:11
  2136.2 31.6 %all-reduce.48.cloned.1.call-done = f32[24,4096]{1,0:T(8,128)} async-done(((f32[24,4096]{1,0:T(8,128)}), f32[24,4096]{1,0:T(8,128)}) %all-reduce.48.cloned.1.call-update) | async-done | bytes 393232 | tf_op jit(solution)/shard_map/psum | solution.py:61
  2169.0 21.4 psum.255
  (424 shorter events, 861.2 us)
Async XLA Ops:
  7.2 134.2 %all-reduce.18.cloned.1.call-start = ((), (), s32[]{:S(2)}) async-start(), calls=%async_computation.1 | async-start | bytes 786432 | tf_op jit(solution)/shard_map/psum | solution.py:40
  67.1 120.5 %all-gather.9.cloned.1.call-start = ((), (), s32[]{:S(2)}) async-start(), calls=%async_computation | async-start | bytes 1769472 | tf_op jit(solution)/shard_map/all_gather | solution.py:11
  67.9 189.6 %all-reduce.20.cloned.1.call-start = ((), (), s32[]{:S(2)}) async-start(), calls=%async_computation.2 | async-start | bytes 786432 | tf_op jit(solution)/shard_map/psum | solution.py:61
  71.8 1790.9 %copy-start.12 = (f32[1,16,2,128]{3,1,2,0:T(8,128)}, f32[1,16,2,128]{3,1,2,0:T(8,128)S(1)}, u32[]{:S(2)}) copy-start(f32[1,16,2,128]{3,1,2,0:T(8,128)S(1)} %copy.24) | copy-start | bytes 49156
  73.1 1789.6 %copy-start.14 = (f32[1,16,2,128]{3,1,2,0:T(8,128)}, f32[1,16,2,128]{3,1,2,0:T(8,128)S(1)}, u32[]{:S(2)}) copy-start(f32[1,16,2,128]{3,1,2,0:T(8,128)S(1)} %copy.28) | copy-start | bytes 49156
  73.2 1789.5 %copy-start.16 = (f32[1,16,2,128]{3,1,2,0:T(8,128)}, f32[1,16,2,128]{3,1,2,0:T(8,128)S(1)}, u32[]{:S(2)}) copy-start(f32[1,16,2,128]{3,1,2,0:T(8,128)S(1)} %copy.22) | copy-start | bytes 49156
  73.3 1789.4 %copy-start.18 = (f32[1,16,2,128]{3,1,2,0:T(8,128)}, f32[1,16,2,128]{3,1,2,0:T(8,128)S(1)}, u32[]{:S(2)}) copy-start(f32[1,16,2,128]{3,1,2,0:T(8,128)S(1)} %copy.26) | copy-start | bytes 49156
  225.9 189.7 %all-reduce.22.cloned.1.call-start = ((), (), s32[]{:S(2)}) async-start(), calls=%async_computation.4 | async-start | bytes 786432 | tf_op jit(solution)/shard_map/psum | solution.py:40
  280.0 292.8 %copy-start.28 = (f32[24]{0:T(128)}, f32[24]{0:T(128)S(1)}, u32[]{:S(2)}) copy-start(f32[24]{0:T(128)S(1)} %div.45) | copy-start | bytes 292
  298.5 274.3 %copy-start.29 = (f32[24]{0:T(128)}, f32[24]{0:T(128)S(1)}, u32[]{:S(2)}) copy-start(f32[24]{0:T(128)S(1)} %div.46) | copy-start | bytes 292
  346.4 115.4 %all-gather.11.cloned.1.call-start = ((), (), s32[]{:S(2)}) async-start(), calls=%async_computation.3 | async-start | bytes 1769472 | tf_op jit(solution)/shard_map/all_gather | solution.py:11
  346.9 184.6 %all-reduce.24.cloned.1.call-start = ((), (), s32[]{:S(2)}) async-start(), calls=%async_computation.5 | async-start | bytes 786432 | tf_op jit(solution)/shard_map/psum | solution.py:61
  500.0 189.1 %all-reduce.26.cloned.1.call-start = ((), (), s32[]{:S(2)}) async-start(), calls=%async_computation.7 | async-start | bytes 786432 | tf_op jit(solution)/shard_map/psum | solution.py:40
  573.0 273.2 %copy-start.4 = (f32[24,4096]{1,0:T(8,128)}, f32[24,4096]{1,0:T(8,128)S(1)}, u32[]{:S(2)}) copy-start(f32[24,4096]{1,0:T(8,128)S(1)} %get-tuple-element.25) | copy-start | bytes 1179652
  619.9 115.5 %all-gather.13.cloned.1.call-start = ((), (), s32[]{:S(2)}) async-start(), calls=%async_computation.6 | async-start | bytes 1769472 | tf_op jit(solution)/shard_map/all_gather | solution.py:11
  620.6 184.5 %all-reduce.28.cloned.1.call-start = ((), (), s32[]{:S(2)}) async-start(), calls=%async_computation.8 | async-start | bytes 786432 | tf_op jit(solution)/shard_map/psum | solution.py:61
  773.5 188.8 %all-reduce.30.cloned.1.call-start = ((), (), s32[]{:S(2)}) async-start(), calls=%async_computation.10 | async-start | bytes 786432 | tf_op jit(solution)/shard_map/psum | solution.py:40
  846.3 272.6 %copy-start.6 = (f32[24,4096]{1,0:T(8,128)}, f32[24,4096]{1,0:T(8,128)S(1)}, u32[]{:S(2)}) copy-start(f32[24,4096]{1,0:T(8,128)S(1)} %get-tuple-element.21) | copy-start | bytes 1179652
  893.2 115.0 %all-gather.15.cloned.1.call-start = ((), (), s32[]{:S(2)}) async-start(), calls=%async_computation.9 | async-start | bytes 1769472 | tf_op jit(solution)/shard_map/all_gather | solution.py:11
  893.9 184.0 %all-reduce.32.cloned.1.call-start = ((), (), s32[]{:S(2)}) async-start(), calls=%async_computation.11 | async-start | bytes 786432 | tf_op jit(solution)/shard_map/psum | solution.py:61
  1046.3 188.7 %all-reduce.34.cloned.1.call-start = ((), (), s32[]{:S(2)}) async-start(), calls=%async_computation.13 | async-start | bytes 786432 | tf_op jit(solution)/shard_map/psum | solution.py:40
  1165.7 114.8 %all-gather.17.cloned.1.call-start = ((), (), s32[]{:S(2)}) async-start(), calls=%async_computation.12 | async-start | bytes 1769472 | tf_op jit(solution)/shard_map/all_gather | solution.py:11
  1166.3 184.0 %all-reduce.36.cloned.1.call-start = ((), (), s32[]{:S(2)}) async-start(), calls=%async_computation.14 | async-start | bytes 786432 | tf_op jit(solution)/shard_map/psum | solution.py:61
  1318.7 188.7 %all-reduce.38.cloned.1.call-start = ((), (), s32[]{:S(2)}) async-start(), calls=%async_computation.16 | async-start | bytes 786432 | tf_op jit(solution)/shard_map/psum | solution.py:40
  1438.2 114.8 %all-gather.19.cloned.1.call-start = ((), (), s32[]{:S(2)}) async-start(), calls=%async_computation.15 | async-start | bytes 1769472 | tf_op jit(solution)/shard_map/all_gather | solution.py:11
  1438.8 183.9 %all-reduce.40.cloned.1.call-start = ((), (), s32[]{:S(2)}) async-start(), calls=%async_computation.17 | async-start | bytes 786432 | tf_op jit(solution)/shard_map/psum | solution.py:61
  1591.1 188.7 %all-reduce.42.cloned.1.call-start = ((), (), s32[]{:S(2)}) async-start(), calls=%async_computation.19 | async-start | bytes 786432 | tf_op jit(solution)/shard_map/psum | solution.py:40
  1710.6 114.8 %all-gather.21.cloned.1.call-start = ((), (), s32[]{:S(2)}) async-start(), calls=%async_computation.18 | async-start | bytes 1769472 | tf_op jit(solution)/shard_map/all_gather | solution.py:11
  1711.2 184.0 %all-reduce.44.cloned.1.call-start = ((), (), s32[]{:S(2)}) async-start(), calls=%async_computation.20 | async-start | bytes 786432 | tf_op jit(solution)/shard_map/psum | solution.py:61
  1863.6 188.3 %all-reduce.46.cloned.1.call-start = ((), (), s32[]{:S(2)}) async-start(), calls=%async_computation.22 | async-start | bytes 786432 | tf_op jit(solution)/shard_map/psum | solution.py:40
  1982.7 115.0 %all-gather.23.cloned.1.call-start = ((), (), s32[]{:S(2)}) async-start(), calls=%async_computation.21 | async-start | bytes 1769472 | tf_op jit(solution)/shard_map/all_gather | solution.py:11
  1983.4 184.3 %all-reduce.48.cloned.1.call-start = ((), (), s32[]{:S(2)}) async-start(), calls=%async_computation.23 | async-start | bytes 786432 | tf_op jit(solution)/shard_map/psum | solution.py:61
  (30 other events, 918.6 us)
Sparse Core Ops, SparseCore 0:
  67.2 74.0 all-reduce.17
  144.3 43.2 all-gather.8
  226.0 31.4 all-reduce.19
  346.5 69.0 all-reduce.21
  418.4 43.2 all-gather.10
  500.1 31.4 all-reduce.23
  620.0 69.0 all-reduce.25
  692.1 43.2 all-gather.12
  773.7 31.4 all-reduce.27
  893.3 69.0 all-reduce.29
  964.8 43.2 all-gather.14
  1046.4 31.4 all-reduce.31
  1165.9 69.0 all-reduce.33
  1237.2 43.2 all-gather.16
  1318.8 31.4 all-reduce.35
  1438.3 69.0 all-reduce.37
  1509.7 43.2 all-gather.18
  1591.3 31.4 all-reduce.39
  1710.7 69.0 all-reduce.41
  1782.1 43.2 all-gather.20
  1863.7 31.4 all-reduce.43
  1982.8 69.0 all-reduce.45
  2054.3 43.2 all-gather.22
  2136.3 31.4 all-reduce.47
where the time goes:
time: 2220 us; the launch traced here: 2200 us
  waiting for transfers between devices  1150 us (52%)
  matrix products  664 us (30%)
  blocking collectives  292 us (13%)
  other arithmetic  50.1 us (2%)
  between operations  28.9 us (1%)
    psum x8, waiting for transfers between devices, kernel_terms(): lax.psum(jnp.stack(forward_list).astype(jnp.bfloat16), 'col')  548 us
    dot_general x64, matrix products, kernel_terms(): lax.dot_general(col_piece, blocks[k, m], (((1,), (1,)), ((), ())), prefer...  366 us
    all_gather x8, waiting for transfers between devices, fetch_rows(): gathered = lax.all_gather(slab_bf, 'col', axis=1, tiled=True)  341 us
    dot_general x64, matrix products, kernel_terms(): jnp.dot(fetched[k], blocks[k, m], preferred_element_type=jnp.float32)  298 us
    psum x15, blocking collectives, slab_total(): return lax.psum(value, 'col')  292 us
    psum x8, waiting for transfers between devices, on_device(): image = noise_var[None, :] * direction + lax.psum(terms, 'row')  252 us
  transfers between devices with their start and end apart: 24, of which 24 were waited for; matrix products, arithmetic and copies ran while one was open for 1% of the time, Pallas kernels for 0%

commit v1 on v0

v1 whole, which is shorter than its diff:
```python
import functools

import jax
import jax.numpy as jnp
from jax import lax
from jax.experimental import pallas as pl
from jax.experimental.pallas import tpu as pltpu
from jax.sharding import PartitionSpec as P

ITERS = 8
RESIDENT = 6
ROWS = 512
STEP = 256
MESH = pl.DeviceIdType.MESH
F32 = jnp.float32
BF16 = jnp.bfloat16


def cg_kernel(
    n_row, n_col, rb, cb, width, resident,
    rows_ref, rhs_ref, noise_ref, k_hbm,
    x_ref, r_ref,
    kres, kbuf, d, dall, vj, vi, facc, fbf, frecv, rsum, macc, th, hrecv, xrecv, im, srecv,
    ksem, bsem, ds, dr, gs, gr, fs, fr, as_, ar, hs, hr, xs, xr, cs, cr, ss, sr,
):
    slots = rb * cb
    slab = cb * width
    half = slab // 2
    chunk = rb * width // n_col
    n_x = n_row // 2
    vectors = rhs_ref.shape[0]
    per = width // ROWS
    streamed = (slots - resident) * per
    held = resident * per
    row = lax.axis_index("row")
    col = lax.axis_index("col")
    core = lax.rem(row, 2)
    xg = row // 2
    mate = row + 1 - 2 * core

    def column(j):
        return lax.rem(col + j, n_col)

    def source(j):
        return lax.rem(col - j + n_col, n_col)

    def x_row(j):
        return lax.rem(xg + j, n_x) * 2 + core

    def x_from(j):
        return lax.rem(xg - j + n_x, n_x)

    def remote(src, dst, send, recv, to):
        return pltpu.make_async_remote_copy(
            src_ref=src, dst_ref=dst, send_sem=send, recv_sem=recv, device_id=to, device_id_type=MESH
        )

    def each(lo, hi, body):
        def step(j, carry):
            body(j)
            return carry

        lax.fori_loop(lo, hi, step, 0)

    def d_send(j):
        at = dall.at[2 * col + core]
        return remote(at, at, ds.at[j], dr.at[j], (row, column(j)))

    def d_recv(j):
        at = dall.at[2 * source(j) + core]
        return remote(at, at, ds.at[j], dr.at[j], (row, column(j)))

    def g_send(j):
        at = dall.at[2 * source(j) + core]
        return remote(at, at, gs.at[j], gr.at[j], (mate, col))

    def g_recv(j):
        at = dall.at[2 * source(j) + 1 - core]
        return remote(at, at, gs.at[j], gr.at[j], (mate, col))

    def f_copy(j):
        return remote(fbf.at[column(j)], frecv.at[j], fs.at[j], fr.at[j], (row, column(j)))

    def a_send(j):
        return remote(rsum.at[col], rsum.at[col], as_.at[j], ar.at[j], (row, column(j)))

    def a_recv(j):
        at = rsum.at[source(j)]
        return remote(at, at, as_.at[j], ar.at[j], (row, column(j)))

    def s_send(j):
        return remote(srecv.at[col], srecv.at[col], ss.at[j], sr.at[j], (row, column(j)))

    def s_recv(j):
        at = srecv.at[source(j)]
        return remote(at, at, ss.at[j], sr.at[j], (row, column(j)))

    def slot_load(s):
        return pltpu.make_async_copy(k_hbm.at[s], kres.at[s], ksem.at[s])

    def stream(i):
        s = resident + i // per
        at = pl.multiple_of(lax.rem(i, per) * ROWS, ROWS)
        b = lax.rem(i, 2)
        return pltpu.make_async_copy(k_hbm.at[s, pl.ds(at, ROWS), :], kbuf.at[b], bsem.at[b])

    barrier = pltpu.get_barrier_semaphore()
    each(1, n_col, lambda j: pl.semaphore_signal(barrier, inc=1, device_id=(row, column(j)), device_id_type=MESH))
    pl.semaphore_signal(barrier, inc=1, device_id=(mate, col), device_id_type=MESH)
    for j in range(1, n_x):
        pl.semaphore_signal(barrier, inc=1, device_id=(x_row(j), col), device_id_type=MESH)

    each(0, resident, lambda s: slot_load(s).start())
    x_ref[...] = jnp.zeros_like(x_ref)
    r_ref[...] = rhs_ref[...]
    d[...] = rhs_ref[...]
    for h in range(2):
        dall[2 * col + h] = d[:, h * half : (h + 1) * half].astype(BF16)
    pl.semaphore_wait(barrier, n_col + n_x - 1)

    def forward(block, s, at):
        k = s // cb
        facc[k, :, pl.ds(at, ROWS)] += lax.dot_general(
            vj[s], block, (((1,), (1,)), ((), ())), preferred_element_type=F32
        )

    def mirror(block, s, at):
        m = lax.rem(s, cb)
        macc[m] += jnp.dot(vi[s, :, pl.ds(at, ROWS)], block, preferred_element_type=F32)

    def over(product, lo, hi, first=None):
        def resident_piece(u):
            s = u // per
            at = pl.multiple_of(lax.rem(u, per) * ROWS, ROWS)
            if first is not None:

                @pl.when(jnp.logical_and(first, lax.rem(u, per) == 0))
                def _():
                    slot_load(s).wait()

            product(kres[s, pl.ds(at, ROWS), :], s, at)

        if streamed == 0:
            each(lo, hi, resident_piece)
            return
        share = held // streamed

        def step(i):
            for q in range(share):
                resident_piece(i * share + q)
            stream(i).wait()
            product(kbuf[lax.rem(i, 2)], resident + i // per, pl.multiple_of(lax.rem(i, per) * ROWS, ROWS))

            @pl.when(i + 2 < streamed)
            def _():
                stream(i + 2).start()

        each(lo, hi, step)

    steps = streamed if streamed else held

    def prefetch():
        if streamed:
            stream(0).start()
            stream(1).start()

    def iteration(t, carry):
        each(1, n_col, lambda j: d_send(j).start())
        facc[...] = jnp.zeros_like(facc)
        macc[...] = jnp.zeros_like(macc)
        prefetch()
        for s in range(slots):
            k, m = s // cb, s % cb
            used = (col * cb + m >= rows_ref[0, k]).astype(F32)
            vj[s] = (d[:, m * width : (m + 1) * width] * used).astype(BF16)
        over(forward, 0, steps, t == 0)
        for c in range(n_col):
            k, at = c * chunk // width, c * chunk % width
            fbf[c] = facc[k, :, at : at + chunk].astype(BF16)
        each(1, n_col, lambda j: f_copy(j).start())
        prefetch()

        def pass_on(j):
            d_recv(j).wait_recv()
            g_send(j).start()

        each(1, n_col, pass_on)
        each(1, n_col, lambda j: g_recv(j).wait_recv())
        pieces = width // half if half < width else 1
        for s in range(slots):
            k, m = s // cb, s % cb
            used = (col * cb + m >= rows_ref[0, k]).astype(F32)
            span = width // pieces
            for p in range(pieces):
                part = dall[rows_ref[0, k] * pieces + p].astype(F32) * used
                vi[s, :, p * span : (p + 1) * span] = part.astype(BF16)
        over(mirror, 0, steps // 2)
        total = fbf[col].astype(F32)
        for j in range(1, n_col):
            f_copy(j).wait_recv()
            total = total + frecv[j].astype(F32)
        rsum[col] = total.astype(BF16)
        each(1, n_col, lambda j: a_send(j).start())
        over(mirror, steps // 2, steps)
        each(1, n_col, lambda j: a_recv(j).wait_recv())

        for h in range(2):
            m, off = h * half // width, h * half % width
            block = col * cb + m
            piece = min(chunk, half)
            for q in range(half // piece):
                at = off + q * piece
                value = macc[m, :, at : at + piece]
                for k in range(rb):
                    c, inner = (k * width + at) // chunk, (k * width + at) % chunk
                    select = (rows_ref[0, k] == block).astype(F32)
                    value = value + rsum[c, :, inner : inner + piece].astype(F32) * select
                th[h, :, q * piece : (q + 1) * piece] = value

        give = remote(th.at[1 - core], hrecv, hs, hr, (mate, col))
        give.start()
        give.wait()
        par = lax.rem(t, 2)
        xrecv[par, xg] = th[core] + hrecv[...]
        for j in range(1, n_x):
            at = xrecv.at[par, xg]
            remote(at, at, xs.at[j], xr.at[par, j], (x_row(j), col)).start()
        for j in range(1, n_x):
            at = xrecv.at[par, x_from(j)]
            remote(at, at, xs.at[j], xr.at[par, j], (x_row(j), col)).wait()
        value = xrecv[par, 0]
        for q in range(1, n_x):
            value = value + xrecv[par, q]
        im[core] = value
        mine, other = im.at[core], im.at[1 - core]
        remote(mine, mine, cs, cr, (mate, col)).start()
        back = remote(other, other, cs, cr, (mate, col))
        back.wait()

        sums = [jnp.zeros((vectors, STEP), F32) for _ in range(4)]
        for q in range(slab // STEP):
            at = q * STEP
            h, inner = at // half, at % half
            dd, rr = d[:, at : at + STEP], r_ref[:, at : at + STEP]
            ii = noise_ref[:, at : at + STEP] * dd + im[h, :, inner : inner + STEP]
            im[h, :, inner : inner + STEP] = ii
            sums = [sums[0] + dd * ii, sums[1] + rr * ii, sums[2] + ii * ii, sums[3] + rr * rr]
        lane = lax.broadcasted_iota(jnp.int32, (vectors, 128), 1)
        pay = jnp.zeros((vectors, 128), F32)
        for q in range(4):
            pay = jnp.where(lane == q, jnp.sum(sums[q], axis=1, keepdims=True), pay)
        srecv[col] = pay
        each(1, n_col, lambda j: g_send(j).wait_send())
        each(1, n_col, lambda j: s_send(j).start())
        each(1, n_col, lambda j: s_recv(j).wait_recv())

        def sent(j):
            d_send(j).wait_send()
            f_copy(j).wait_send()
            a_send(j).wait_send()
            s_send(j).wait_send()

        each(1, n_col, sent)
        total = srecv[0]
        for q in range(1, n_col):
            total = total + srecv[q]
        curvature, cross, square, norm = [total[:, q : q + 1] for q in range(4)]
        alpha = norm / curvature
        after = norm - 2.0 * alpha * cross + alpha * alpha * square
        beta = after / norm
        for q in range(slab // STEP):
            at = q * STEP
            h, inner = at // half, at % half
            dd = d[:, at : at + STEP]
            x_ref[:, at : at + STEP] += alpha * dd
            rr = r_ref[:, at : at + STEP] - alpha * im[h, :, inner : inner + STEP]
            r_ref[:, at : at + STEP] = rr
            dd = rr + beta * dd
            d[:, at : at + STEP] = dd
            dall[2 * col + h, :, inner : inner + STEP] = dd.astype(BF16)
        return carry

    lax.fori_loop(0, ITERS, iteration, 0)


def on_device(n_row, n_col, rhs, noise_var, block_rows, kernel_blocks):
    rb, cb, width = kernel_blocks.shape[2], kernel_blocks.shape[3], kernel_blocks.shape[4]
    vectors, slab = rhs.shape
    slots, half, chunk, n_x = rb * cb, slab // 2, rb * width // n_col, n_row // 2
    resident = min(RESIDENT, slots)
    dma = pltpu.SemaphoreType.DMA
    vmem = pl.BlockSpec(memory_space=pltpu.VMEM)
    return pl.pallas_call(
        functools.partial(cg_kernel, n_row, n_col, rb, cb, width, resident),
        out_shape=[jax.ShapeDtypeStruct((vectors, slab), F32)] * 2,
        in_specs=[pl.BlockSpec(memory_space=pltpu.SMEM), vmem, vmem, pl.BlockSpec(memory_space=pl.ANY)],
        out_specs=[vmem, vmem],
        scratch_shapes=[
            pltpu.VMEM((resident, width, width), BF16),
            pltpu.VMEM((2, ROWS, width), BF16),
            pltpu.VMEM((vectors, slab), F32),
            pltpu.VMEM((2 * n_col, vectors, half), BF16),
            pltpu.VMEM((slots, vectors, width), BF16),
            pltpu.VMEM((slots, vectors, width), BF16),
            pltpu.VMEM((rb, vectors, width), F32),
            pltpu.VMEM((n_col, vectors, chunk), BF16),
            pltpu.VMEM((n_col, vectors, chunk), BF16),
            pltpu.VMEM((n_col, vectors, chunk), BF16),
            pltpu.VMEM((cb, vectors, width), F32),
            pltpu.VMEM((2, vectors, half), F32),
            pltpu.VMEM((vectors, half), F32),
            pltpu.VMEM((2, n_x, vectors, half), F32),
            pltpu.VMEM((2, vectors, half), F32),
            pltpu.VMEM((n_col, vectors, 128), F32),
            dma((resident,)), dma((2,)),
            dma((n_col,)), dma((n_col,)),
            dma((n_col,)), dma((n_col,)),
            dma((n_col,)), dma((n_col,)),
            dma((n_col,)), dma((n_col,)),
            dma, dma,
            dma((n_x,)), dma((2, n_x)),
            dma, dma,
            dma((n_col,)), dma((n_col,)),
        ],
        compiler_params=pltpu.CompilerParams(
            collective_id=0, has_side_effects=True, vmem_limit_bytes=63 * 1024 * 1024
        ),
        cost_estimate=pl.CostEstimate(
            flops=ITERS * slots * 4 * vectors * width * width,
            bytes_accessed=slots * width * width * 2,
            transcendentals=0,
        ),
    )(block_rows, rhs, noise_var.reshape(1, slab), kernel_blocks.reshape(slots, width, width))


def solution(mesh):
    return jax.shard_map(
        functools.partial(on_device, mesh.shape["row"], mesh.shape["col"]),
        mesh=mesh,
        in_specs=(P(None, "col"), P("col"), P("row", None), P("row", "col", None, None, None, None)),
        out_specs=(P(None, "col"), P(None, "col")),
        check_vma=False,
    )
```

time: 2220 us -> 485 us (0.22)
  waiting for transfers between devices: 1150 us -> 0 us
  matrix products: 664 us -> 0 us
  Pallas kernels: 0 us -> 481 us
  blocking collectives: 292 us -> 0 us
  other arithmetic: 50.1 us -> 0 us
  between operations: 28.9 us -> 0.64 us
    psum x16 -> x0, waiting for transfers between devices: 800 us -> none  [the longest x8 548 us: kernel_terms(): lax.psum(jnp.stack(forward_list).astype(jnp.bfloat16), 'col')]
    dot_general x128 -> x0, matrix products: 664 us -> none  [the longest x64 366 us: kernel_terms(): lax.dot_general(col_piece, blocks[k, m], (((1,), (1,)), ((), ())), prefer...]
    pallas_call x0 -> x1, Pallas kernels: none -> 481 us  [on_device(): pl.pallas_call(functools.partial(cg_kernel, n_row, n_col, rb, cb, width,...]
    all_gather x8 -> x0, waiting for transfers between devices: 341 us -> none  [fetch_rows(): gathered = lax.all_gather(slab_bf, 'col', axis=1, tiled=True)]
    psum x15 -> x0, blocking collectives: 292 us -> none  [slab_total(): return lax.psum(value, 'col')]
  transfers between devices with their start and end apart: 24 -> 0, of which waited for: 24 -> 0; matrix products, arithmetic and copies ran while one was open for 1% -> 0% of each run, Pallas kernels for 0% -> 0%
where the time goes in v1:
time: 485 us
  Pallas kernels  481 us (99%)
    pallas_call x1, Pallas kernels, on_device(): pl.pallas_call(functools.partial(cg_kernel, n_row, n_col, rb, cb, width,...  481 us

profile of v1, /device:TPU:0, one launch (start us, length us, event | category | flops | bytes accessed | tf_op | source)
XLA Modules:
  0.0 484.8 jit_solution(12349999209205472227)
XLA Ops:
  0.6 480.7 %shard_map.59 = (f32[24,4096]{1,0:T(8,128)}, f32[24,4096]{1,0:T(8,128)}) custom-call(s32[1,4]{1,0:T(1,128)} %rows_ref.1, f32[24,4096]{1,0:T(8,128)} %rhs_ref.1, f32[1,4096]{1,0:T(1,128)} %bitcast.2, bf16[8,2048,2048]{2,1,0:T(8,128)(2,1)} %bitcast.1.k_hbm), custom_call_target="tpu_custom_call" | custom-call | flops 25769803776 | bytes 67108864 | tf_op jit(solution)/shard_map/pallas_call | solution.py:293
  481.3 1.8 copy.8
  483.1 1.8 copy.9

commit v2 on v1

--- a/solution.py
+++ b/solution.py
@@ -128,7 +128,7 @@
         m = lax.rem(s, cb)
         macc[m] += jnp.dot(vi[s, :, pl.ds(at, ROWS)], block, preferred_element_type=F32)
 
-    def over(product, lo, hi, first=None):
+    def over(product, lo, hi, first=None, beside=None):
         def resident_piece(u):
             s = u // per
             at = pl.multiple_of(lax.rem(u, per) * ROWS, ROWS)
@@ -141,7 +141,13 @@
             product(kres[s, pl.ds(at, ROWS), :], s, at)
 
         if streamed == 0:
-            each(lo, hi, resident_piece)
+
+            def only(i):
+                resident_piece(i)
+                if beside is not None:
+                    beside(i)
+
+            each(lo, hi, only)
             return
         share = held // streamed
 
@@ -154,6 +160,9 @@
             @pl.when(i + 2 < streamed)
             def _():
                 stream(i + 2).start()
+
+            if beside is not None:
+                beside(i)
 
         each(lo, hi, step)
 
@@ -173,18 +182,21 @@
             k, m = s // cb, s % cb
             used = (col * cb + m >= rows_ref[0, k]).astype(F32)
             vj[s] = (d[:, m * width : (m + 1) * width] * used).astype(BF16)
-        over(forward, 0, steps, t == 0)
+
+        def pass_on(j):
+            d_recv(j).wait_recv()
+            g_send(j).start()
+
+        def share_out(i):
+            each(1 + (n_col - 1) * i // steps, 1 + (n_col - 1) * (i + 1) // steps, pass_on)
+
+        over(forward, 0, steps, t == 0, share_out)
         for c in range(n_col):
             k, at = c * chunk // width, c * chunk % width
             fbf[c] = facc[k, :, at : at + chunk].astype(BF16)
         each(1, n_col, lambda j: f_copy(j).start())
         prefetch()
 
-        def pass_on(j):
-            d_recv(j).wait_recv()
-            g_send(j).start()
-
-        each(1, n_col, pass_on)
         each(1, n_col, lambda j: g_recv(j).wait_recv())
         pieces = width // half if half < width else 1
         for s in range(slots):
@@ -221,16 +233,16 @@
         give.start()
         give.wait()
         par = lax.rem(t, 2)
-        xrecv[par, xg] = th[core] + hrecv[...]
+        xrecv[par, xg] = (th[core] + hrecv[...]).astype(BF16)
         for j in range(1, n_x):
             at = xrecv.at[par, xg]
             remote(at, at, xs.at[j], xr.at[par, j], (x_row(j), col)).start()
         for j in range(1, n_x):
             at = xrecv.at[par, x_from(j)]
             remote(at, at, xs.at[j], xr.at[par, j], (x_row(j), col)).wait()
-        value = xrecv[par, 0]
+        value = xrecv[par, 0].astype(F32)
         for q in range(1, n_x):
-            value = value + xrecv[par, q]
+            value = value + xrecv[par, q].astype(F32)
         im[core] = value
         mine, other = im.at[core], im.at[1 - core]
         remote(mine, mine, cs, cr, (mate, col)).start()
@@ -309,7 +321,7 @@
             pltpu.VMEM((cb, vectors, width), F32),
             pltpu.VMEM((2, vectors, half), F32),
             pltpu.VMEM((vectors, half), F32),
-            pltpu.VMEM((2, n_x, vectors, half), F32),
+            pltpu.VMEM((2, n_x, vectors, half), BF16),
             pltpu.VMEM((2, vectors, half), F32),
             pltpu.VMEM((n_col, vectors, 128), F32),
             dma((resident,)), dma((2,)),

time: 485 us -> 479 us (0.988)
  Pallas kernels: 481 us -> 474 us
    pallas_call x1, Pallas kernels: 481 us -> 474 us  [on_device(): pl.pallas_call(functools.partial(cg_kernel, n_row, n_col, rb, cb, width,...]
where the time goes in v2:
time: 479 us
  Pallas kernels  474 us (99%)
    pallas_call x1, Pallas kernels, on_device(): pl.pallas_call(functools.partial(cg_kernel, n_row, n_col, rb, cb, width,...  474 us

profile of v2, /device:TPU:0, one launch (start us, length us, event | category | flops | bytes accessed | tf_op | source)
XLA Modules:
  0.0 478.6 jit_solution(3460041890896209148)
XLA Ops:
  0.6 474.4 %shard_map.59 = (f32[24,4096]{1,0:T(8,128)}, f32[24,4096]{1,0:T(8,128)}) custom-call(s32[1,4]{1,0:T(1,128)} %rows_ref.1, f32[24,4096]{1,0:T(8,128)} %rhs_ref.1, f32[1,4096]{1,0:T(1,128)} %bitcast.2, bf16[8,2048,2048]{2,1,0:T(8,128)(2,1)} %bitcast.1.k_hbm), custom_call_target="tpu_custom_call" | custom-call | flops 25769803776 | bytes 67108864 | tf_op jit(solution)/shard_map/pallas_call | solution.py:305
  475.0 1.8 copy.8
  476.8 1.8 copy.9
